TPU v7x, 32 devices: a whole 2x2x4 slice. The times are simulated.
32 devices in a mesh: ctx: 8 (over z, core), exp: 4 (over y, x).
Axes of the slice: x: 2, y: 2, z: 4, core: 2. Of those that a mesh axis runs over, the one named last changes fastest.
Arguments:
- queries: bfloat16 [1024, 6144], P('ctx', 'exp'), may hold values from -12 to 12
- keys_values: bfloat16 [1024, 8, 256], P('ctx', 'exp'), may hold values from -12 to 12
- doc_ids: int32 [1024], P('ctx'), may hold values from 0 to 7, never falling along the last dimension, each value on 1 to 768 neighbouring positions
- gate_up: bfloat16 [4, 640, 16384], P('exp', None, 'ctx'), may hold values from -6 to 6
- down_weight: bfloat16 [4, 16384, 6144], P('exp', 'ctx'), may hold values from -0.046875 to 0.046875
- routes: int32 [1024, 2], P(('ctx', 'exp')), may hold values from 0 to 3, all different within a row; in each aligned block of 32 rows (0 to 31, 32 to 63, ...) at most 20 rows name the same one
- route_weights: float32 [1024, 2], P(('ctx', 'exp')), may hold values from 0.1 to 1
Outputs:
- context: bfloat16 [1024, 6144], P('ctx', 'exp')
- moe_out: bfloat16 [1024, 6144], P(('ctx', 'exp'))
Inputs may be any that keep to these rules, and one draw needn't show every extreme that they name: doc_ids never falls along the sequence; each document has 1 to 768 tokens and one has exactly 768. `routes`: the 2 experts of a token differ; among the 32 tokens of one device (aligned blocks) no expert is named more than 20 times, a bound that some block reaches.
All inputs are finite; a program needn't handle non-finite values.
Results may differ from a plain program's by a relative error of at most 0.025.
Values may be sent and summed in bfloat16 or wider, within the bound.
A program may use at most 128 MiB of HBM per device.

v0:
```python
import math

import jax
import jax.numpy as jnp
from jax import lax
from jax.sharding import PartitionSpec as P


def shards(queries, keys_values, doc_ids, gate_up, down_weight, routes, route_weights):
    tok_rows = queries.shape[0]
    local_heads = keys_values.shape[1]
    head_size = keys_values.shape[2] // 2
    groups = queries.shape[1] // (local_heads * head_size)
    query_grid = queries.reshape(tok_rows, local_heads, groups, head_size)
    first_pos = lax.axis_index("ctx") * tok_rows
    query_pos = first_pos + jnp.arange(tok_rows, dtype=jnp.int32)
    scale = 1.0 / math.sqrt(head_size)
    doc_wire = doc_ids.astype(jnp.bfloat16)
    kv_piece = lax.all_gather(keys_values, "ctx", axis=0, tiled=True)
    doc_piece = lax.all_gather(doc_wire, "ctx", axis=0, tiled=True)
    count = kv_piece.shape[0]
    key_pos = jnp.arange(count, dtype=jnp.int32)
    scores = (
        jnp.einsum(
            "qhgd,khd->hgqk",
            query_grid,
            kv_piece[:, :, :head_size],
            preferred_element_type=jnp.float32,
        )
        * scale
    )
    allowed = (doc_ids[:, None] == doc_piece.astype(jnp.int32)[None, :]) & (
        key_pos[None, :] <= query_pos[:, None]
    )
    scores = jnp.where(allowed, scores, jnp.float32(-1e30))
    run_max = jnp.full((local_heads, groups, tok_rows), -1e30, jnp.float32)
    new_max = jnp.maximum(run_max, jnp.max(scores, axis=-1))
    weights = jnp.where(allowed, jnp.exp(scores - new_max[..., None]), jnp.float32(0.0))
    new_total = jnp.sum(weights, axis=-1)
    update = jnp.einsum(
        "hgqk,khd->qhgd",
        weights.astype(jnp.bfloat16),
        kv_piece[:, :, head_size:],
        preferred_element_type=jnp.float32,
    )
    context = (
        (update / jnp.transpose(new_total, (2, 0, 1))[..., None])
        .reshape(tok_rows, -1)
        .astype(jnp.bfloat16)
    )
    residual = lax.all_to_all(context, "exp", split_axis=0, concat_axis=1, tiled=True)
    acts = gate_up[0]
    weight = down_weight[0]
    slot_total = acts.shape[0]
    ctx_count = lax.axis_size("ctx")
    exp_count = lax.axis_size("exp")
    capacity = slot_total // (ctx_count * exp_count)
    width = weight.shape[1]
    mine = lax.psum_scatter(
        jnp.dot(acts, weight, preferred_element_type=jnp.float32).astype(jnp.bfloat16),
        "ctx",
        scatter_dimension=0,
        tiled=True,
    ).astype(jnp.float32)
    mine = mine.astype(jnp.bfloat16).reshape(exp_count, capacity, width)
    home_rows = lax.all_to_all(mine, "exp", split_axis=0, concat_axis=0, tiled=True)
    expert_count = home_rows.shape[0]
    flat_routes = routes.reshape(-1)
    onehot = (flat_routes[:, None] == jnp.arange(expert_count, dtype=jnp.int32)[None, :]).astype(
        jnp.int32
    )
    earlier = jnp.cumsum(onehot, axis=0) - onehot
    slot_index = jnp.sum(earlier * onehot, axis=1)
    row_index = flat_routes * capacity + slot_index
    picked = home_rows.reshape(expert_count * capacity, width)[row_index]
    picked = picked.reshape(routes.shape[0], routes.shape[1], width).astype(jnp.float32)
    mixed = jnp.sum(route_weights[:, :, None] * picked, axis=1)
    moe_out = (residual.astype(jnp.float32) + mixed).astype(jnp.bfloat16)
    return (context, moe_out)


def solution(mesh):
    in_specs = (
        P("ctx", "exp"),
        P("ctx", "exp", None),
        P("ctx"),
        P("exp", None, "ctx"),
        P("exp", "ctx", None),
        P(("ctx", "exp"), None),
        P(("ctx", "exp"), None),
    )
    out_specs = (P("ctx", "exp"), P(("ctx", "exp"), None))
    return jax.shard_map(shards, mesh=mesh, in_specs=in_specs, out_specs=out_specs, check_vma=False)
```

profile of v0, /device:TPU:1, one launch (start us, length us, event | category | flops | bytes accessed | tf_op | source)
XLA Modules:
  0.0 159.7 jit_solution(2815178357742431849)
XLA Ops:
  7.2 1.7 %copy.39 = bf16[128,2,256]{2,0,1:T(8,128)(2,1)} copy(bf16[128,2,256]{2,1,0:T(2,128)(2,1)} %param.8) | data formatting | bytes 262144 | tf_op args[1]
  9.0 21.6 %fusion.2 = bf16[640,6144]{1,0:T(8,128)(2,1)} fusion(bf16[1,2048,6144]{2,1,0:T(8,128)(2,1)} %param.11, bf16[1,640,2048]{2,1,0:T(8,128)(2,1)S(1)} %copy-done), kind=kOutput, calls=%fused_computation.3 | convolution fusion | flops 16110059520 | bytes 35651584 | tf_op jit(solution)/shard_map/dot_general | solution.py:60
  30.7 0.6 copy-done.5
  31.3 13.2 %all-gather = bf16[8,1,128]{2,1,0:T(2,128)(2,1)S(1)} all-gather(bf16[1,1,128]{2,1,0:T(2,128)(2,1)S(1)} %convert_bitcast_fusion.1), channel_id=1, replica_groups=mesh['ctx'=8,'exp'=4] {'ctx'}, dimensions={0}, use_global_device_ids=true | all-gather | bytes 2304 | tf_op jit(solution)/shard_map/all_gather | solution.py:20
  44.5 0.6 convert_element_type.62
  45.1 0.2 copy.40
  45.4 0.1 copy.47
  45.5 0.6 mul.46
  46.1 0.7 eq.31
  46.9 0.9 fusion.22
  47.9 2.1 %fusion.5 = (f32[2,6,128]{2,1,0:T(8,128)S(1)}, f32[2,1024,128,6]{2,1,3,0:T(8,128)S(1)}) fusion(pred[128,1024]{0,1:T(8,128)(4,1)S(1)} %fusion.22, bf16[128,2,6,128]{0,3,2,1:T(8,128)(2,1)S(1)} %bitcast.61, bf16[1024,2,256]{2,0,1:T(8,128)(2,1)} %all-gather.3.cloned.1.call-done), kind=kOutput, calls=%fused_computation.6 | convolution fusion | flops 407370240 | bytes 7346176 | tf_op jit(solution)/shard_map/qhgd,khd->hgqk/dot_general | solution.py:24
  50.0 1.5 fusion.6
  51.6 1.6 %fusion.18 = bf16[128,2,6,128]{0,3,2,1:T(8,128)(2,1)S(1)} fusion(f32[2,1024,128,6]{2,1,3,0:T(8,128)S(1)} %get-tuple-element.11, f32[2,6,128]{2,1,0:T(8,128)S(1)} %broadcast_maximum_fusion, pred[128,1024]{0,1:T(8,128)(4,1)S(1)} %fusion.22, bf16[1024,2,256]{2,0,1:T(8,128)(2,1)S(1)} %copy-done.2, f32[128,2,6]{0,2,1:T(8,128)S(1)} %bitcast.64), kind=kOutput, calls=%fused_computation.15 | convolution fusion | flops 410910720 | bytes 7356416 | tf_op jit(solution)/shard_map/hgqk,khd->qhgd/dot_general | solution.py:40
  53.2 0.4 copy.44
  53.6 1.2 convert_element_type.50
  54.8 3.5 %all-to-all-start = ((bf16[4,32,1536]{2,1,0:T(8,128)(2,1)}), bf16[4,32,1536]{2,1,0:T(8,128)(2,1)S(1)}, u32[]{:S(2)}, u32[]{:S(2)}) async-start(bf16[4,32,1536]{2,1,0:T(8,128)(2,1)} %convert_element_type.50), calls=%async_computation | async-start | bytes 786432 | tf_op jit(solution)/shard_map/all_to_all | solution.py:51
  58.3 0.8 fusion.23
  59.0 0.1 reduce_window_sum.11
  59.1 0.9 select_reduce_fusion
  60.0 58.9 %reduce-scatter.2.cloned.1.call-done = bf16[80,6144]{1,0:T(8,128)(2,1)} async-done(((bf16[640,6144]{1,0:T(8,128)(2,1)}), bf16[80,6144]{1,0:T(8,128)(2,1)}) %reduce-scatter.2.cloned.1.call-update) | async-done | bytes 983056 | tf_op jit(solution)/shard_map/reduce_scatter | solution.py:59
  118.9 2.2 %reshape.67 = bf16[4,20,6144]{2,1,0:T(8,128)(2,1)} reshape(bf16[80,6144]{1,0:T(8,128)(2,1)} %reduce-scatter.2.cloned.1.call-done) | data formatting | bytes 1966080 | tf_op jit(solution)/shard_map/reshape | solution.py:65
  121.1 4.4 %all-to-all-start.1 = ((bf16[4,20,6144]{2,1,0:T(8,128)(2,1)}), bf16[4,20,6144]{2,1,0:T(8,128)(2,1)}, u32[]{:S(2)}, u32[]{:S(2)}) async-start(bf16[4,20,6144]{2,1,0:T(8,128)(2,1)} %reshape.67), calls=%async_computation.2 | async-start | bytes 2359296 | tf_op jit(solution)/shard_map/all_to_all | solution.py:66
  125.5 0.6 fusion.24
  126.2 0.6 pad_clamp_fusion
  126.8 0.9 copy.49
  127.8 1.0 copy.56
  128.7 11.2 %all-to-all-done.1 = bf16[4,20,6144]{2,1,0:T(8,128)(2,1)} async-done(((bf16[4,20,6144]{2,1,0:T(8,128)(2,1)}), bf16[4,20,6144]{2,1,0:T(8,128)(2,1)}, u32[]{:S(2)}, u32[]{:S(2)}) %all-to-all-start.1) | async-done | bytes 983072 | tf_op jit(solution)/shard_map/all_to_all | solution.py:66
  139.9 2.2 %reshape.68 = bf16[80,6144]{1,0:T(8,128)(2,1)} reshape(bf16[4,20,6144]{2,1,0:T(8,128)(2,1)} %all-to-all-done.1) | data formatting | bytes 1966080 | tf_op jit(solution)/shard_map/reshape | solution.py:75
  142.1 3.2 %gather_fusion = bf16[64,6144]{1,0:T(8,128)(2,1)S(1)} fusion(bf16[80,6144]{1,0:T(8,128)(2,1)} %reshape.68, s32[1024]{0:T(1024)} %pad_clamp_fusion), kind=kCustom, calls=%fused_computation | custom fusion | bytes 1573120 | tf_op jit(solution)/shard_map/gather | solution.py:75
  145.3 2.1 %reshape.70 = f32[32,2,6144]{2,1,0:T(2,128)} reshape(bf16[64,6144]{1,0:T(8,128)(2,1)S(1)} %gather_fusion) | data formatting | bytes 2359296 | tf_op jit(solution)/shard_map/convert_element_type | solution.py:76
  147.4 3.5 %multiply_reduce_fusion = f32[32,6144]{1,0:T(8,128)S(1)} fusion(f32[32,2,6144]{2,1,0:T(2,128)} %reshape.70, f32[32,2]{1,0:T(8,128)S(1)} %copy.46), kind=kLoop, calls=%fused_computation.12 | loop fusion | flops 589824 | bytes 2359552 | tf_op jit(solution)/shard_map/reduce_sum | solution.py:77
  150.9 1.9 %add_convert_fusion = bf16[32,6144]{1,0:T(8,128)(2,1)} fusion(f32[32,6144]{1,0:T(8,128)} %bitcast.60, f32[32,6144]{1,0:T(8,128)S(1)} %multiply_reduce_fusion), kind=kLoop, calls=%fused_computation.17 | loop fusion | flops 393216 | bytes 1966080 | tf_op jit(solution)/shard_map/convert_element_type | solution.py:78
  (24 shorter events, 0.4 us)
Async XLA Ops:
  7.2 1.9 %copy-start = (bf16[1,640,2048]{2,1,0:T(8,128)(2,1)S(1)}, bf16[1,640,2048]{2,1,0:T(8,128)(2,1)}, u32[]{:S(2)}) copy-start(bf16[1,640,2048]{2,1,0:T(8,128)(2,1)} %param.10) | copy-start | bytes 7864324
  7.2 40.7 %all-gather.3.cloned.1.call-start = ((), (), s32[]{:S(2)}) async-start(), calls=%async_computation.3 | async-start | bytes 1179648 | tf_op jit(solution)/shard_map/all_gather | solution.py:19
  9.0 109.9 %reduce-scatter.2.cloned.1.call-start = ((), (), s32[]{:S(2)}) async-start(), calls=%async_computation.4 | async-start | bytes 8847360 | tf_op jit(solution)/shard_map/reduce_scatter | solution.py:59
  30.6 0.7 copy-start.5
  30.6 14.5 %copy-start.1 = (bf16[128,1536]{1,0:T(8,128)(2,1)S(1)}, bf16[128,1536]{1,0:T(8,128)(2,1)}, u32[]{:S(2)}) copy-start(bf16[128,1536]{1,0:T(8,128)(2,1)} %param.7) | copy-start | bytes 1179652
  30.6 14.7 %copy-start.3 = (s32[32,2]{0,1:T(2,128)S(1)}, s32[32,2]{0,1:T(2,128)}, u32[]{:S(2)}) copy-start(s32[32,2]{0,1:T(2,128)} %param.12) | copy-start | bytes 772
  30.6 16.2 %copy-start.4 = (f32[32,2]{0,1:T(2,128)S(1)}, f32[32,2]{0,1:T(2,128)}, u32[]{:S(2)}) copy-start(f32[32,2]{0,1:T(2,128)} %param.13) | copy-start | bytes 772
  47.9 3.7 %copy-start.2 = (bf16[1024,2,256]{2,0,1:T(8,128)(2,1)S(1)}, bf16[1024,2,256]{2,0,1:T(8,128)(2,1)}, u32[]{:S(2)}) copy-start(bf16[1024,2,256]{2,0,1:T(8,128)(2,1)} %all-gather.3.cloned.1.call-done) | copy-start | bytes 3145732
  54.8 66.3 %all-to-all-start = ((bf16[4,32,1536]{2,1,0:T(8,128)(2,1)}), bf16[4,32,1536]{2,1,0:T(8,128)(2,1)S(1)}, u32[]{:S(2)}, u32[]{:S(2)}) async-start(bf16[4,32,1536]{2,1,0:T(8,128)(2,1)} %convert_element_type.50), calls=%async_computation | async-start | bytes 786432 | tf_op jit(solution)/shard_map/all_to_all | solution.py:51
  121.1 18.8 %all-to-all-start.1 = ((bf16[4,20,6144]{2,1,0:T(8,128)(2,1)}), bf16[4,20,6144]{2,1,0:T(8,128)(2,1)}, u32[]{:S(2)}, u32[]{:S(2)}) async-start(bf16[4,20,6144]{2,1,0:T(8,128)(2,1)} %reshape.67), calls=%async_computation.2 | async-start | bytes 2359296 | tf_op jit(solution)/shard_map/all_to_all | solution.py:66
Sparse Core Ops, SparseCore 0:
  10.2 24.5 all-gather.2
  37.1 81.7 reduce-scatter.1
where the time goes:
time: 162 us; the launch traced here: 160 us
  waiting for transfers between devices  70.1 us (43%)
  matrix products  25.4 us (16%)
  local copies, waits for them, and re-layouts  17.4 us (11%)
  between operations  14.2 us (9%)
  blocking collectives  13.2 us (8%)
  other arithmetic  11.5 us (7%)
  starting transfers between devices  7.98 us (5%)
    reduce_scatter x1, waiting for transfers between devices, shards(): lax.psum_scatter(jnp.dot(acts, weight, preferred_element_type=jnp.float32...  58.9 us
    dot_general x1, matrix products, shards(): jnp.dot(acts, weight, preferred_element_type=jnp.float32)  21.6 us
    all_gather x1, blocking collectives, shards(): doc_piece = lax.all_gather(doc_wire, 'ctx', axis=0, tiled=True)  13.2 us
    all_to_all x1, waiting for transfers between devices, shards(): lax.all_to_all(mine, 'exp', split_axis=0, concat_axis=0, tiled=True)  11.2 us
    all_to_all x1, starting transfers between devices, shards(): lax.all_to_all(mine, 'exp', split_axis=0, concat_axis=0, tiled=True)  4.44 us
    unnamed x17, local copies, waits for them, and re-layouts  3.68 us
    reduce_sum x1, other arithmetic, shards(): mixed = jnp.sum(route_weights[:, :, None] * picked, axis=1)  3.51 us
    all_to_all x1, starting transfers between devices, shards(): lax.all_to_all(context, 'exp', split_axis=0, concat_axis=1, tiled=True)  3.46 us
  transfers between devices with their start and end apart: 4, of which 2 were waited for; matrix products, arithmetic and copies ran while one was open for 24% of the time, Pallas kernels for 0%

commit v1 on v0

v1 whole, which is shorter than its diff:
```python
import functools
import math

import jax
import jax.numpy as jnp
from jax import lax
from jax.experimental import pallas as pl
from jax.experimental.pallas import tpu as pltpu
from jax.sharding import PartitionSpec as P

MESH = pl.DeviceIdType.MESH
BF16 = jnp.bfloat16
F32 = jnp.float32
COLS = 512
WEIGHT_SLOTS = 4
DOC_ROWS = 16


def iota(shape, dim):
    return lax.broadcasted_iota(jnp.int32, shape, dim).astype(F32)


def whole_part(x, size):
    return jnp.floor((x + 0.5) * (1.0 / size))


def kernel(
    n_ctx, n_exp, steps,
    q_hbm, kv_ref, doc_ref, acts_hbm, w_hbm, routes_ref, rw_ref,
    ctx_ref, out_ref,
    q_buf, kv_buf, mask_buf, acts, acts_p, wbuf, csend, crecv, own, rows, mix_c, mix_w,
    zs, zr, fs, mixed, resid,
    in_sem, w_sem, c_ssem, c_rsem, x_ssem, x_rsem, z_ssem, z_rsem, f_ssem, f_rsem,
    k_ssem, k_rsem, p_ssem, p_rsem, m_ssem, m_rsem, r_ssem, r_rsem,
):
    ctx = lax.axis_index("ctx")
    exp = lax.axis_index("exp")
    core = lax.rem(ctx, 2)
    chip = lax.div(ctx, 2)
    mate = ctx + 1 - 2 * core
    n_chip = n_ctx // 2
    slots, depth = acts.shape
    group = slots // n_exp
    cap = group // n_ctx
    tok = routes_ref.shape[0]
    seq_rows = kv_ref.shape[0]
    half_cols = w_hbm.shape[2] // 2
    cols = COLS

    def w_copy(j):
        side = lax.rem(j + 1 + core, 2)
        start = pl.multiple_of(side * half_cols + lax.div(j, 2) * cols, 128)
        slot = lax.rem(j, WEIGHT_SLOTS)
        return pltpu.make_async_copy(
            w_hbm.at[0, :, pl.ds(start, cols)], wbuf.at[slot], w_sem.at[slot]
        )

    acts_copy = pltpu.make_async_copy(acts_hbm.at[0], acts, in_sem.at[0])
    q_copy = pltpu.make_async_copy(q_hbm, q_buf, in_sem.at[1])
    acts_copy.start()
    for j in range(WEIGHT_SLOTS):
        w_copy(jnp.int32(j)).start()
    q_copy.start()

    barrier = pltpu.get_barrier_semaphore()
    for d in range(1, n_ctx):
        pl.semaphore_signal(
            barrier, inc=1, device_id=(lax.rem(ctx + d, n_ctx), exp), device_id_type=MESH
        )
    for d in range(1, n_exp):
        pl.semaphore_signal(
            barrier, inc=1, device_id=(ctx, lax.rem(exp + d, n_exp)), device_id_type=MESH
        )

    kv_buf[ctx, 0:seq_rows, :] = kv_ref[...]
    doc_row = doc_ref[...].astype(F32)
    kv_buf[ctx, seq_rows:, 0:seq_rows] = jnp.broadcast_to(
        doc_row, (DOC_ROWS, seq_rows)
    ).astype(BF16)
    for i in range(n_chip):
        @pl.when(i > chip)
        def _():
            kv_buf[2 * i] = jnp.zeros(kv_buf.shape[1:], BF16)
            kv_buf[2 * i + 1] = jnp.zeros(kv_buf.shape[1:], BF16)

    wide = mix_c.shape[2]
    col = iota((tok, wide), 1)
    col_exp = whole_part(col, cap)
    col_slot = col - col_exp * cap
    is0 = routes_ref[:, 0:1].astype(F32) == col_exp
    is1 = routes_ref[:, 1:2].astype(F32) == col_exp
    named = jnp.where(is0 | is1, 1.0, 0.0).astype(BF16)
    before = jnp.where(iota((tok, tok), 1) < iota((tok, tok), 0), 1.0, 0.0).astype(BF16)
    earlier = jnp.dot(before, named, preferred_element_type=F32)
    gate = jnp.where(is0, rw_ref[:, 0:1], 0.0) + jnp.where(is1, rw_ref[:, 1:2], 0.0)
    mix_c[ctx] = jnp.where(earlier == col_slot, gate, 0.0).astype(BF16)

    def core_copy(s):
        return pltpu.make_async_remote_copy(
            csend.at[s], crecv.at[s], c_ssem.at[s], c_rsem.at[s],
            device_id=(mate, exp), device_id_type=MESH,
        )

    def rows_of(e):
        return pl.ds(pl.multiple_of(e * group, 16), group)

    def exp_copy(s, d, source=None):
        peer = lax.rem(exp + d, n_exp)
        source = exp if source is None else source
        return pltpu.make_async_remote_copy(
            crecv.at[s, rows_of(peer), :], rows.at[s, rows_of(source), :],
            x_ssem.at[s, d], x_rsem.at[s, source],
            device_id=(ctx, peer), device_id_type=MESH,
        )

    def z_copy(s, d, source=None):
        peer = lax.rem(chip + d, n_chip)
        source = chip if source is None else source
        return pltpu.make_async_remote_copy(
            zs.at[s, pl.ds(pl.multiple_of(peer * 2 * tok, 16), 2 * tok), :],
            zr.at[s, source], z_ssem.at[s, d], z_rsem.at[s, source],
            device_id=(2 * peer + core, exp), device_id_type=MESH,
        )

    def final_copy(s, side):
        return pltpu.make_async_remote_copy(
            fs.at[s], mixed.at[side, s], f_ssem.at[s], f_rsem.at[s],
            device_id=(mate, exp), device_id_type=MESH,
        )

    def kv_copy(d, source=None):
        source = chip if source is None else source
        block = kv_buf.at[2 * source + core]
        return pltpu.make_async_remote_copy(
            block, block, k_ssem.at[d], k_rsem.at[source],
            device_id=(lax.rem(ctx + 2 * d, n_ctx), exp), device_id_type=MESH,
        )

    def mate_copy(i, side):
        block = kv_buf.at[2 * i + side]
        return pltpu.make_async_remote_copy(
            block, block, p_ssem.at[i], p_rsem.at[i],
            device_id=(mate, exp), device_id_type=MESH,
        )

    def mix_copy(d, source=None):
        source = ctx if source is None else source
        return pltpu.make_async_remote_copy(
            mix_c.at[source], mix_c.at[source], m_ssem.at[d], m_rsem.at[source],
            device_id=(lax.rem(ctx + d, n_ctx), exp), device_id_type=MESH,
        )

    def resid_copy(d, source=None):
        peer = lax.rem(exp + d, n_exp)
        source = exp if source is None else source
        return pltpu.make_async_remote_copy(
            ctx_ref.at[pl.ds(pl.multiple_of(peer * tok, 16), tok), :], resid.at[source],
            r_ssem.at[d], r_rsem.at[source],
            device_id=(ctx, peer), device_id_type=MESH,
        )

    pl.semaphore_wait(barrier, n_ctx - 1 + n_exp - 1)
    mate_copy(chip, core).start()
    for d in range(1, n_chip):
        @pl.when(chip + d < n_chip)
        def _():
            kv_copy(d).start()
    for d in range(1, n_ctx):
        mix_copy(d).start()

    acts_copy.wait()
    place = iota((slots, 128), 0)
    place_exp = whole_part(place, group)
    place_rest = place - place_exp * group
    place_ctx = whole_part(place_rest, cap)
    came = (place_ctx * n_exp + place_exp) * cap + place_rest - place_ctx * cap
    order = jnp.where(iota((slots, slots), 1) == came[:, 0:1], 1.0, 0.0).astype(BF16)

    @pl.loop(0, depth // 512)
    def _(i):
        at = pl.ds(pl.multiple_of(i * 512, 128), 512)
        acts_p[:, at] = jnp.dot(order, acts[:, at], preferred_element_type=F32).astype(BF16)

    @pl.loop(0, steps)
    def _(s):
        for side in range(2):
            j = 2 * s + side
            w_copy(j).wait()
            product = jnp.dot(
                acts_p[...], wbuf[lax.rem(j, WEIGHT_SLOTS)], preferred_element_type=F32
            )
            if side == 0:
                csend[s] = product.astype(BF16)
                core_copy(s).start()
            else:
                own[...] = product

            @pl.when(j + WEIGHT_SLOTS < 2 * steps)
            def _():
                w_copy(j + WEIGHT_SLOTS).start()
        core_copy(s).wait_recv()
        crecv[s] = (own[...] + crecv[s].astype(F32)).astype(BF16)
        for d in range(1, n_exp):
            exp_copy(s, d).start()
        rows[s, rows_of(exp), :] = crecv[s, rows_of(exp), :]

    for d in range(1, n_ctx):
        mix_copy(d, lax.rem(ctx + d, n_ctx)).wait_recv()
    total_tok = n_ctx * tok
    at = iota((8, slots), 1)
    at_exp = whole_part(at, group)
    at_rest = at - at_exp * group
    at_ctx = whole_part(at_rest, cap)
    at_slot = at_exp * cap + at_rest - at_ctx * cap
    spread = jnp.where(iota((wide, slots), 0) == at_slot[0:1, :], 1.0, 0.0).astype(BF16)
    spread_w = jnp.dot(
        mix_c[...].reshape(total_tok, wide), spread, preferred_element_type=F32
    )
    token_ctx = whole_part(iota((total_tok, 128), 0), tok)[:, 0:1]
    mix_w[...] = jnp.where(token_ctx == at_ctx[0:1, :], spread_w, 0.0).astype(BF16)

    def combine(s):
        for d in range(1, n_exp):
            exp_copy(s, d, lax.rem(exp + d, n_exp)).wait_recv()
        zs[s] = jnp.dot(mix_w[...], rows[s], preferred_element_type=F32).astype(BF16)
        for d in range(1, n_chip):
            z_copy(s, d).start()

    def finish(s):
        for d in range(1, n_chip):
            z_copy(s, d, lax.rem(chip + d, n_chip)).wait_recv()

        def total_of(k):
            first = pl.multiple_of((2 * chip + k) * tok, 16)
            total = zs[s, pl.ds(first, tok), :].astype(F32)
            for d in range(1, n_chip):
                peer = lax.rem(chip + d, n_chip)
                part = zr[s, peer, pl.ds(pl.multiple_of(k * tok, 16), tok), :]
                total = total + part.astype(F32)
            return total.astype(BF16)

        fs[s] = total_of(1 - core)
        final_copy(s, core).start()
        mixed[core, s] = total_of(core)

    for i in range(n_chip - 1):
        @pl.when(i < chip)
        def _():
            kv_copy(1, i).wait_recv()
            mate_copy(i, core).start()
    combine(0)
    q_copy.wait()
    for i in range(n_chip):
        @pl.when(i <= chip)
        def _():
            mate_copy(i, 1 - core).wait_recv()

    seq = n_ctx * seq_rows
    key_doc = jnp.concatenate(
        [kv_buf[i, seq_rows:, 0:seq_rows].astype(F32)[0:1, :] for i in range(n_ctx)], axis=1
    )
    query_doc = jnp.broadcast_to(doc_row, (seq_rows, seq_rows)).T[:, 0:1]
    query_pos = lax.broadcasted_iota(jnp.int32, (seq_rows, seq), 0) + ctx * seq_rows
    key_pos = lax.broadcasted_iota(jnp.int32, (seq_rows, seq), 1)
    mask_buf[...] = jnp.where((query_doc == key_doc) & (key_pos <= query_pos), 0.0, -1e30)
    kv_heads = kv_ref.shape[1] // 256
    groups = q_buf.shape[1] // (kv_heads * 128)
    scale = 1.0 / math.sqrt(128)
    for g in range(kv_heads):
        @pl.loop(0, groups)
        def _(h):
            at = pl.ds(pl.multiple_of((g * groups + h) * 128, 128), 128)
            keys = kv_buf[:, 0:seq_rows, g * 256:g * 256 + 128].reshape(seq, 128)
            values = kv_buf[:, 0:seq_rows, g * 256 + 128:g * 256 + 256].reshape(seq, 128)
            scores = lax.dot_general(
                q_buf[:, at], keys, (((1,), (1,)), ((), ())), preferred_element_type=F32
            ) * scale + mask_buf[...]
            weights = jnp.exp(scores - jnp.max(scores, axis=1, keepdims=True))
            total = jnp.sum(weights, axis=1, keepdims=True)
            summed = jnp.dot(weights.astype(BF16), values, preferred_element_type=F32)
            ctx_ref[:, at] = (summed / total).astype(BF16)

    for d in range(1, n_exp):
        resid_copy(d).start()
    resid[exp] = ctx_ref[pl.ds(pl.multiple_of(exp * tok, 16), tok), :]

    @pl.loop(1, steps)
    def _(s):
        combine(s)
        finish(s - 1)

    finish(steps - 1)
    for d in range(1, n_exp):
        resid_copy(d, lax.rem(exp + d, n_exp)).wait_recv()
    for s in range(steps):
        final_copy(s, 1 - core).wait_recv()

    part = resid.shape[2]
    piece = math.gcd(cols, part)
    for first in range(0, 2 * half_cols, piece):
        side, rest = divmod(first, half_cols)
        s, off = divmod(rest, cols)
        e, inner = divmod(first, part)
        out_ref[:, first:first + piece] = (
            resid[e, :, inner:inner + piece].astype(F32)
            + mixed[side, s, :, off:off + piece].astype(F32)
        ).astype(BF16)

    @pl.loop(0, steps)
    def _(s):
        core_copy(s).wait_send()
        final_copy(s, core).wait_send()
        for d in range(1, n_exp):
            exp_copy(s, d).wait_send()
        for d in range(1, n_chip):
            z_copy(s, d).wait_send()

    for d in range(1, n_exp):
        resid_copy(d).wait_send()
    for d in range(1, n_ctx):
        mix_copy(d).wait_send()
    for i in range(n_chip):
        @pl.when(i <= chip)
        def _():
            mate_copy(i, core).wait_send()
    for d in range(1, n_chip):
        @pl.when(chip + d < n_chip)
        def _():
            kv_copy(d).wait_send()


def shards(n_ctx, n_exp, queries, keys_values, doc_ids, gate_up, down_weight, routes, route_weights):
    rows_q, width_q = queries.shape
    slots, depth = gate_up.shape[1:]
    width = down_weight.shape[2]
    tok = routes.shape[0]
    half = width // 2
    steps = half // COLS
    n_chip = n_ctx // 2
    cap = slots // (n_ctx * n_exp)
    wide = -(-n_exp * cap // 128) * 128
    kv = keys_values.reshape(rows_q, -1)
    dma = pltpu.SemaphoreType.DMA
    vmem = pl.BlockSpec(memory_space=pltpu.VMEM)
    hbm = pl.BlockSpec(memory_space=pl.ANY)
    return pl.pallas_call(
        functools.partial(kernel, n_ctx, n_exp, steps),
        out_shape=(
            jax.ShapeDtypeStruct((rows_q, width_q), BF16),
            jax.ShapeDtypeStruct((tok, width), BF16),
        ),
        in_specs=[hbm, vmem, vmem, hbm, hbm, vmem, vmem],
        out_specs=(vmem, vmem),
        scratch_shapes=[
            pltpu.VMEM((rows_q, width_q), BF16),
            pltpu.VMEM((n_ctx, rows_q + DOC_ROWS, kv.shape[1]), BF16),
            pltpu.VMEM((rows_q, n_ctx * rows_q), F32),
            pltpu.VMEM((slots, depth), BF16),
            pltpu.VMEM((slots, depth), BF16),
            pltpu.VMEM((WEIGHT_SLOTS, depth, COLS), BF16),
            pltpu.VMEM((steps, slots, COLS), BF16),
            pltpu.VMEM((steps, slots, COLS), BF16),
            pltpu.VMEM((slots, COLS), F32),
            pltpu.VMEM((steps, slots, COLS), BF16),
            pltpu.VMEM((n_ctx, tok, wide), BF16),
            pltpu.VMEM((n_ctx * tok, slots), BF16),
            pltpu.VMEM((steps, n_ctx * tok, COLS), BF16),
            pltpu.VMEM((steps, n_chip, 2 * tok, COLS), BF16),
            pltpu.VMEM((steps, tok, COLS), BF16),
            pltpu.VMEM((2, steps, tok, COLS), BF16),
            pltpu.VMEM((n_exp, tok, width_q), BF16),
            dma((2,)),
            dma((WEIGHT_SLOTS,)),
            dma((steps,)),
            dma((steps,)),
            dma((steps, n_exp)),
            dma((steps, n_exp)),
            dma((steps, n_chip)),
            dma((steps, n_chip)),
            dma((steps,)),
            dma((steps,)),
            dma((n_chip,)),
            dma((n_chip,)),
            dma((n_chip,)),
            dma((n_chip,)),
            dma((n_ctx,)),
            dma((n_ctx,)),
            dma((n_exp,)),
            dma((n_exp,)),
        ],
        compiler_params=pltpu.CompilerParams(
            collective_id=0, has_side_effects=True, vmem_limit_bytes=60 * 2**20
        ),
    )(queries, kv, doc_ids.reshape(1, -1), gate_up, down_weight, routes, route_weights)


def solution(mesh):
    in_specs = (
        P("ctx", "exp"),
        P("ctx", "exp", None),
        P("ctx"),
        P("exp", None, "ctx"),
        P("exp", "ctx", None),
        P(("ctx", "exp"), None),
        P(("ctx", "exp"), None),
    )
    out_specs = (P("ctx", "exp"), P(("ctx", "exp"), None))
    body = functools.partial(shards, mesh.shape["ctx"], mesh.shape["exp"])
    return jax.shard_map(body, mesh=mesh, in_specs=in_specs, out_specs=out_specs, check_vma=False)
```

time: 162 us -> 79.9 us (0.49); the launches traced: 160 us -> 79.6 us
  Pallas kernels: 0 us -> 71.1 us
  waiting for transfers between devices: 70.1 us -> 0 us
  matrix products: 25.4 us -> 0 us
  between operations: 14.2 us -> 0.64 us
  blocking collectives: 13.2 us -> 0 us
  other arithmetic: 11.5 us -> 0 us
  local copies, waits for them, and re-layouts: 17.4 us -> 7.83 us
  starting transfers between devices: 7.98 us -> 0 us
    pallas_call x0 -> x1, Pallas kernels: none -> 71.1 us  [shards(): pl.pallas_call(functools.partial(kernel, n_ctx, n_exp, steps), out_shape=...]
    reduce_scatter x1 -> x0, waiting for transfers between devices: 58.9 us -> none  [shards(): lax.psum_scatter(jnp.dot(acts, weight, preferred_element_type=jnp.float32...]
    dot_general x3 -> x0, matrix products: 25.4 us -> none  [the longest x1 21.6 us: shards(): jnp.dot(acts, weight, preferred_element_type=jnp.float32)]
    all_gather x1 -> x0, blocking collectives: 13.2 us -> none  [shards(): doc_piece = lax.all_gather(doc_wire, 'ctx', axis=0, tiled=True)]
    all_to_all x2 -> x0, waiting for transfers between devices: 11.2 us -> none  [the longest x1 11.2 us: shards(): lax.all_to_all(mine, 'exp', split_axis=0, concat_axis=0, tiled=True)]
    all_to_all x2 -> x0, starting transfers between devices: 7.9 us -> none  [the longest x1 4.44 us: shards(): lax.all_to_all(mine, 'exp', split_axis=0, concat_axis=0, tiled=True)]
    reduce_sum x3 -> x0, other arithmetic: 5.88 us -> none  [the longest x1 3.51 us: shards(): mixed = jnp.sum(route_weights[:, :, None] * picked, axis=1)]
    convert_element_type x4 -> x0, local copies, waits for them, and re-layouts: 4.68 us -> none  [the longest x1 2.12 us: shards(): picked.reshape(routes.shape[0], routes.shape[1], width).astype(jnp.float32)]
  transfers between devices with their start and end apart: 4 -> 0, of which waited for: 2 -> 0; matrix products, arithmetic and copies ran while one was open for 24% -> 0% of each run, Pallas kernels for 0% -> 0%
where the time goes in v1:
time: 79.9 us; the launch traced here: 79.6 us
  Pallas kernels  71.1 us (89%)
  local copies, waits for them, and re-layouts  7.83 us (10%)
    pallas_call x1, Pallas kernels, shards(): pl.pallas_call(functools.partial(kernel, n_ctx, n_exp, steps), out_shape=...  71.1 us
    unnamed x5, local copies, waits for them, and re-layouts  7.83 us

profile of v1, /device:TPU:1, one launch (start us, length us, event | category | flops | bytes accessed | tf_op | source)
XLA Modules:
  0.0 79.6 jit_solution(17639811158460259282)
XLA Ops:
  0.6 1.4 %copy.9.routes_ref = s32[32,2]{1,0:T(8,128)} copy(s32[32,2]{0,1:T(2,128)} %param.12) | data formatting | bytes 512 | tf_op args[5]
  2.0 1.4 %copy.10.rw_ref = f32[32,2]{1,0:T(8,128)} copy(f32[32,2]{0,1:T(2,128)} %param.13) | data formatting | bytes 512 | tf_op args[6]
  3.3 1.6 %copy.11 = bf16[16,8,2,256]{3,1,2,0:T(8,128)(2,1)} copy(bf16[16,8,2,256]{3,2,1,0:T(2,128)(2,1)} %bitcast.4) | data formatting | bytes 262144
  4.9 71.1 %shard_map.86 = (bf16[128,1536]{1,0:T(8,128)(2,1)}, bf16[32,6144]{1,0:T(8,128)(2,1)}) custom-call(bf16[128,1536]{1,0:T(8,128)(2,1)} %q_hbm.1, bf16[128,512]{1,0:T(8,128)(2,1)} %bitcast.3, s32[1,128]{1,0:T(1,128)} %bitcast.5, bf16[1,640,2048]{2,1,0:T(8,128)(2,1)} %acts_hbm.1, bf16[1,2048,6144]{2,1,0:T(8,128)(2,1)} %w_hbm.1, s32[32,2]{1,0:T(8,128)} %copy.9.routes_ref, ...), custom_call_target="tpu_custom_call" | custom-call | tf_op jit(solution)/shard_map/pallas_call | solution.py:346
  76.1 1.8 %copy.14 = bf16[128,1536]{1,0:T(8,128)(2,1)} copy(bf16[128,1536]{1,0:T(8,128)(2,1)} %get-tuple-element.4) | data formatting | bytes 786432
  77.8 1.8 %copy.15 = bf16[32,6144]{1,0:T(8,128)(2,1)} copy(bf16[32,6144]{1,0:T(8,128)(2,1)} %get-tuple-element.5) | data formatting | bytes 786432

commit v2 on v1

--- a/solution.py
+++ b/solution.py
@@ -11,8 +11,8 @@
 MESH = pl.DeviceIdType.MESH
 BF16 = jnp.bfloat16
 F32 = jnp.float32
-COLS = 512
-WEIGHT_SLOTS = 4
+COLS = 256
+WEIGHT_SLOTS = 6
 DOC_ROWS = 16
 
 
@@ -42,7 +42,7 @@
     slots, depth = acts.shape
     group = slots // n_exp
     cap = group // n_ctx
-    tok = routes_ref.shape[0]
+    tok = routes_ref.shape[1]
     seq_rows = kv_ref.shape[0]
     half_cols = w_hbm.shape[2] // 2
     cols = COLS
@@ -72,7 +72,8 @@
             barrier, inc=1, device_id=(ctx, lax.rem(exp + d, n_exp)), device_id_type=MESH
         )
 
-    kv_buf[ctx, 0:seq_rows, :] = kv_ref[...]
+    for g in range(kv_ref.shape[1]):
+        kv_buf[ctx, 0:seq_rows, g * 256:(g + 1) * 256] = kv_ref[:, g, :]
     doc_row = doc_ref[...].astype(F32)
     kv_buf[ctx, seq_rows:, 0:seq_rows] = jnp.broadcast_to(
         doc_row, (DOC_ROWS, seq_rows)
@@ -87,12 +88,19 @@
     col = iota((tok, wide), 1)
     col_exp = whole_part(col, cap)
     col_slot = col - col_exp * cap
-    is0 = routes_ref[:, 0:1].astype(F32) == col_exp
-    is1 = routes_ref[:, 1:2].astype(F32) == col_exp
+
+    def upright(row):
+        same = iota((tok, tok), 0) == iota((tok, tok), 1)
+        return jnp.sum(jnp.where(same, row, 0.0), axis=1, keepdims=True)
+
+    is0 = upright(routes_ref[0:1, :].astype(F32)) == col_exp
+    is1 = upright(routes_ref[1:2, :].astype(F32)) == col_exp
     named = jnp.where(is0 | is1, 1.0, 0.0).astype(BF16)
     before = jnp.where(iota((tok, tok), 1) < iota((tok, tok), 0), 1.0, 0.0).astype(BF16)
     earlier = jnp.dot(before, named, preferred_element_type=F32)
-    gate = jnp.where(is0, rw_ref[:, 0:1], 0.0) + jnp.where(is1, rw_ref[:, 1:2], 0.0)
+    gate = jnp.where(is0, upright(rw_ref[0:1, :]), 0.0) + jnp.where(
+        is1, upright(rw_ref[1:2, :]), 0.0
+    )
     mix_c[ctx] = jnp.where(earlier == col_slot, gate, 0.0).astype(BF16)
 
     def core_copy(s):
@@ -180,6 +188,29 @@
     def _(i):
         at = pl.ds(pl.multiple_of(i * 512, 128), 512)
         acts_p[:, at] = jnp.dot(order, acts[:, at], preferred_element_type=F32).astype(BF16)
+
+    def prepare():
+        for d in range(1, n_ctx):
+            mix_copy(d, lax.rem(ctx + d, n_ctx)).wait_recv()
+        total_tok = n_ctx * tok
+        at = iota((8, slots), 1)
+        at_exp = whole_part(at, group)
+        at_rest = at - at_exp * group
+        at_ctx = whole_part(at_rest, cap)
+        at_slot = at_exp * cap + at_rest - at_ctx * cap
+        spread = jnp.where(iota((wide, slots), 0) == at_slot[0:1, :], 1.0, 0.0).astype(BF16)
+        spread_w = jnp.dot(
+            mix_c[...].reshape(total_tok, wide), spread, preferred_element_type=F32
+        )
+        token_ctx = whole_part(iota((total_tok, 128), 0), tok)[:, 0:1]
+        mix_w[...] = jnp.where(token_ctx == at_ctx[0:1, :], spread_w, 0.0).astype(BF16)
+
+    def combine(s):
+        for d in range(1, n_exp):
+            exp_copy(s, d, lax.rem(exp + d, n_exp)).wait_recv()
+        zs[s] = jnp.dot(mix_w[...], rows[s], preferred_element_type=F32).astype(BF16)
+        for d in range(1, n_chip):
+            z_copy(s, d).start()
 
     @pl.loop(0, steps)
     def _(s):
@@ -204,27 +235,13 @@
             exp_copy(s, d).start()
         rows[s, rows_of(exp), :] = crecv[s, rows_of(exp), :]
 
-    for d in range(1, n_ctx):
-        mix_copy(d, lax.rem(ctx + d, n_ctx)).wait_recv()
-    total_tok = n_ctx * tok
-    at = iota((8, slots), 1)
-    at_exp = whole_part(at, group)
-    at_rest = at - at_exp * group
-    at_ctx = whole_part(at_rest, cap)
-    at_slot = at_exp * cap + at_rest - at_ctx * cap
-    spread = jnp.where(iota((wide, slots), 0) == at_slot[0:1, :], 1.0, 0.0).astype(BF16)
-    spread_w = jnp.dot(
-        mix_c[...].reshape(total_tok, wide), spread, preferred_element_type=F32
-    )
-    token_ctx = whole_part(iota((total_tok, 128), 0), tok)[:, 0:1]
-    mix_w[...] = jnp.where(token_ctx == at_ctx[0:1, :], spread_w, 0.0).astype(BF16)
-
-    def combine(s):
-        for d in range(1, n_exp):
-            exp_copy(s, d, lax.rem(exp + d, n_exp)).wait_recv()
-        zs[s] = jnp.dot(mix_w[...], rows[s], preferred_element_type=F32).astype(BF16)
-        for d in range(1, n_chip):
-            z_copy(s, d).start()
+        @pl.when(s == 2)
+        def _():
+            prepare()
+
+        @pl.when((s >= 3) & (lax.rem(s, 3) != 1))
+        def _():
+            combine(lax.div(2 * s, 3) - 2)
 
     def finish(s):
         for d in range(1, n_chip):
@@ -248,7 +265,6 @@
         def _():
             kv_copy(1, i).wait_recv()
             mate_copy(i, core).start()
-    combine(0)
     q_copy.wait()
     for i in range(n_chip):
         @pl.when(i <= chip)
@@ -263,9 +279,10 @@
     query_pos = lax.broadcasted_iota(jnp.int32, (seq_rows, seq), 0) + ctx * seq_rows
     key_pos = lax.broadcasted_iota(jnp.int32, (seq_rows, seq), 1)
     mask_buf[...] = jnp.where((query_doc == key_doc) & (key_pos <= query_pos), 0.0, -1e30)
-    kv_heads = kv_ref.shape[1] // 256
+    kv_heads = kv_ref.shape[1]
     groups = q_buf.shape[1] // (kv_heads * 128)
     scale = 1.0 / math.sqrt(128)
+    done = 2 * (steps - 1) // 3 - 1
     for g in range(kv_heads):
         @pl.loop(0, groups)
         def _(h):
@@ -280,16 +297,24 @@
             summed = jnp.dot(weights.astype(BF16), values, preferred_element_type=F32)
             ctx_ref[:, at] = (summed / total).astype(BF16)
 
+        if g == 0:
+            @pl.loop(done, done + 2)
+            def _(s):
+                combine(s)
+
     for d in range(1, n_exp):
         resid_copy(d).start()
     resid[exp] = ctx_ref[pl.ds(pl.multiple_of(exp * tok, 16), tok), :]
 
-    @pl.loop(1, steps)
+    @pl.loop(done + 2, steps)
     def _(s):
         combine(s)
-        finish(s - 1)
-
-    finish(steps - 1)
+        finish(s - done - 2)
+
+    @pl.loop(steps - done - 2, steps)
+    def _(s):
+        finish(s)
+
     for d in range(1, n_exp):
         resid_copy(d, lax.rem(exp + d, n_exp)).wait_recv()
     for s in range(steps):
@@ -329,6 +354,15 @@
             kv_copy(d).wait_send()
 
 
+def place_results(ctx_in, out_in, ctx_out, out_out, sem):
+    first = pltpu.make_async_copy(ctx_in, ctx_out, sem.at[0])
+    second = pltpu.make_async_copy(out_in, out_out, sem.at[1])
+    first.start()
+    second.start()
+    first.wait()
+    second.wait()
+
+
 def shards(n_ctx, n_exp, queries, keys_values, doc_ids, gate_up, down_weight, routes, route_weights):
     rows_q, width_q = queries.shape
     slots, depth = gate_up.shape[1:]
@@ -339,11 +373,11 @@
     n_chip = n_ctx // 2
     cap = slots // (n_ctx * n_exp)
     wide = -(-n_exp * cap // 128) * 128
-    kv = keys_values.reshape(rows_q, -1)
+    kv_width = keys_values.shape[1] * keys_values.shape[2]
     dma = pltpu.SemaphoreType.DMA
     vmem = pl.BlockSpec(memory_space=pltpu.VMEM)
     hbm = pl.BlockSpec(memory_space=pl.ANY)
-    return pl.pallas_call(
+    results = pl.pallas_call(
         functools.partial(kernel, n_ctx, n_exp, steps),
         out_shape=(
             jax.ShapeDtypeStruct((rows_q, width_q), BF16),
@@ -353,7 +387,7 @@
         out_specs=(vmem, vmem),
         scratch_shapes=[
             pltpu.VMEM((rows_q, width_q), BF16),
-            pltpu.VMEM((n_ctx, rows_q + DOC_ROWS, kv.shape[1]), BF16),
+            pltpu.VMEM((n_ctx, rows_q + DOC_ROWS, kv_width), BF16),
             pltpu.VMEM((rows_q, n_ctx * rows_q), F32),
             pltpu.VMEM((slots, depth), BF16),
             pltpu.VMEM((slots, depth), BF16),
@@ -391,7 +425,17 @@
         compiler_params=pltpu.CompilerParams(
             collective_id=0, has_side_effects=True, vmem_limit_bytes=60 * 2**20
         ),
-    )(queries, kv, doc_ids.reshape(1, -1), gate_up, down_weight, routes, route_weights)
+    )(
+        queries, keys_values, doc_ids.reshape(1, -1), gate_up, down_weight,
+        routes.T, route_weights.T,
+    )
+    return pl.pallas_call(
+        place_results,
+        out_shape=tuple(jax.ShapeDtypeStruct(r.shape, r.dtype) for r in results),
+        in_specs=[hbm, hbm],
+        out_specs=(hbm, hbm),
+        scratch_shapes=[dma((2,))],
+    )(*results)
 
 
 def solution(mesh):

time: 79.9 us -> 105 us (1.31)
  Pallas kernels: 71.1 us -> 105 us
  local copies, waits for them, and re-layouts: 7.83 us -> 0 us
    pallas_call x0 -> x1, Pallas kernels: none -> 24.9 us  [shards(): pl.pallas_call(place_results, out_shape=tuple((jax.ShapeDtypeStruct(r.sha...]
    pallas_call x1, Pallas kernels: 71.1 us -> 79.7 us  [shards(): pl.pallas_call(functools.partial(kernel, n_ctx, n_exp, steps), out_shape=...]
    unnamed x5 -> x0, local copies, waits for them, and re-layouts: 7.83 us -> none
where the time goes in v2:
time: 105 us
  Pallas kernels  105 us (100%)
    pallas_call x1, Pallas kernels, shards(): pl.pallas_call(functools.partial(kernel, n_ctx, n_exp, steps), out_shape=...  79.7 us
    pallas_call x1, Pallas kernels, shards(): pl.pallas_call(place_results, out_shape=tuple((jax.ShapeDtypeStruct(r.sha...  24.9 us

profile of v2, /device:TPU:1, one launch (start us, length us, event | category | flops | bytes accessed | tf_op | source)
XLA Modules:
  0.0 105.3 jit_solution(4593694262572333448)
XLA Ops:
  0.6 79.7 %shard_map.86 = (bf16[128,1536]{1,0:T(8,128)(2,1)}, bf16[32,6144]{1,0:T(8,128)(2,1)}) custom-call(bf16[128,1536]{1,0:T(8,128)(2,1)} %q_hbm.1, bf16[128,2,256]{2,1,0:T(2,128)(2,1)} %kv_ref.1, s32[1,128]{1,0:T(1,128)} %bitcast.5, bf16[1,640,2048]{2,1,0:T(8,128)(2,1)} %acts_hbm.1, bf16[1,2048,6144]{2,1,0:T(8,128)(2,1)} %w_hbm.1, s32[2,32]{1,0:T(2,128)} %bitcast.3, ...), custom_call_target="tpu_custom_call" | custom-call | tf_op jit(solution)/shard_map/pallas_call | solution.py:380
  80.3 24.9 %shard_map.87 = (bf16[128,1536]{1,0:T(8,128)(2,1)}, bf16[32,6144]{1,0:T(8,128)(2,1)}) custom-call(bf16[128,1536]{1,0:T(8,128)(2,1)} %get-tuple-element.4.ctx_in, bf16[32,6144]{1,0:T(8,128)(2,1)} %get-tuple-element.5.out_in), custom_call_target="tpu_custom_call" | custom-call | tf_op jit(solution)/shard_map/pallas_call | solution.py:432
